TPU v7x, 32 devices: a whole 2x2x4 slice. The times are simulated.
32 devices in a mesh: samp: 16 (over z, y, core), par: 2 (over x).
Axes of the slice: x: 2, y: 2, z: 4, core: 2. Of those that a mesh axis runs over, the one named last changes fastest.
Arguments:
- jacobian: float32 [4096, 8192], P('samp', 'par'), may hold values from -60 to 60, as said below
Outputs:
- gram: float32 [4096, 4096], P('samp', 'par')
Inputs may be any that keep to these rules, and one draw needn't show every extreme that they name: `jacobian`: real-valued log-derivatives.
All inputs are finite; a program needn't handle non-finite values.
Results may differ from a plain program's by a relative error of at most 0.000065.
Values sent between devices are 32-bit elements; how exact they have to be, the bound alone decides.
A program may use at most 128 MiB of HBM per device.

v0:
```python
import jax
import jax.numpy as jnp
from jax import lax
from jax.sharding import PartitionSpec as P


def tile_product(left, right):
    return jnp.dot(
        left, right.T, preferred_element_type=jnp.float32, precision=lax.Precision.HIGHEST
    )


def per_device(jacobian):
    rows = jacobian.shape[0]
    count = lax.axis_size("samp")
    samples = rows * count
    totals = lax.psum(jnp.sum(jacobian, axis=0), "samp")
    centred = jacobian - (totals / samples)[None, :]
    partial_rows = tile_product(centred, lax.all_gather(centred, "samp", axis=0, tiled=True))
    summed = lax.psum_scatter(partial_rows, "par", scatter_dimension=1, tiled=True)
    return summed / samples


def solution(mesh):
    placed = (P("samp", "par"),)
    return jax.shard_map(
        per_device, mesh=mesh, in_specs=placed, out_specs=P("samp", "par"), check_vma=False
    )
```

profile of v0, /device:TPU:29, one launch (start us, length us, event | category | flops | bytes accessed | tf_op | source)
XLA Modules:
  0.0 527.3 jit_solution(13131558636923475280)
XLA Ops:
  6.5 0.0 all-gather.2.cloned.1.call-start
  6.5 2.4 reduce_sum.9
  8.9 57.0 %psum.7 = f32[4096]{0:T(1024)S(1)} all-reduce(f32[4096]{0:T(1024)S(1)} %reduce_sum.9), channel_id=1, replica_groups=mesh['samp'=16,'par'=2] {'samp'}, use_global_device_ids=true, to_apply=%region_1.0 | all-reduce | flops 4096 | bytes 32768 | tf_op jit(solution)/shard_map/psum | solution.py:17
  65.9 4.7 broadcast_subtract_fusion
  70.6 0.0 all-gather.2.cloned.1.call-update
  70.7 0.0 reduce-scatter.2.cloned.1.call-start
  70.7 327.2 %all-gather.2.cloned.1.call-done = f32[4096,4096]{1,0:T(8,128)} async-done(((f32[256,4096]{1,0:T(8,128)}), f32[4096,4096]{1,0:T(8,128)}) %all-gather.2.cloned.1.call-update) | async-done | bytes 67108880 | tf_op jit(solution)/shard_map/all_gather | solution.py:19
  397.9 64.5 %fusion = f32[256,4096]{1,0:T(8,128)} fusion(f32[256,4096]{1,0:T(8,128)} %broadcast_subtract_fusion, f32[4096,4096]{1,0:T(8,128)} %all-gather.2.cloned.1.call-done), kind=kOutput, calls=%fused_computation.3 | convolution fusion | flops 51539607552 | bytes 75497472 | tf_op jit(solution)/shard_map/dot_general | solution.py:8
  462.4 0.0 reduce-scatter.2.cloned.1.call-update
  462.4 55.0 %reduce-scatter.2.cloned.1.call-done = f32[256,2048]{1,0:T(8,128)} async-done(((f32[256,4096]{1,0:T(8,128)}), f32[256,2048]{1,0:T(8,128)}) %reduce-scatter.2.cloned.1.call-update) | async-done | bytes 2097168 | tf_op jit(solution)/shard_map/reduce_scatter | solution.py:20
  517.3 3.1 broadcast_multiply_fusion
  (1 shorter events, 0.0 us)
Async XLA Ops:
  6.5 391.3 %all-gather.2.cloned.1.call-start = ((), (), s32[]{:S(2)}) async-start(), calls=%async_computation.1 | async-start | bytes 71303168 | tf_op jit(solution)/shard_map/all_gather | solution.py:19
  70.7 446.7 %reduce-scatter.2.cloned.1.call-start = ((), (), s32[]{:S(2)}) async-start(), calls=%async_computation.2 | async-start | bytes 6291456 | tf_op jit(solution)/shard_map/reduce_scatter | solution.py:20
Sparse Core Ops, SparseCore 0:
  70.8 327.0 all-gather.1
  462.5 54.7 reduce-scatter.1
where the time goes:
time: 529 us; the launch traced here: 527 us
  waiting for transfers between devices  382 us (72%)
  matrix products  64.5 us (12%)
  blocking collectives  57 us (11%)
  between operations  13.4 us (3%)
  other arithmetic  10.3 us (2%)
    all_gather x1, waiting for transfers between devices, per_device(): lax.all_gather(centred, 'samp', axis=0, tiled=True)  327 us
    dot_general x1, matrix products, tile_product(): jnp.dot(left, right.T, preferred_element_type=jnp.float32, precision=lax....  64.5 us
    psum x1, blocking collectives, per_device(): totals = lax.psum(jnp.sum(jacobian, axis=0), 'samp')  57 us
    reduce_scatter x1, waiting for transfers between devices, per_device(): lax.psum_scatter(partial_rows, 'par', scatter_dimension=1, tiled=True)  55 us
  transfers between devices with their start and end apart: 2, of which 2 were waited for; matrix products, arithmetic and copies ran while one was open for 0% of the time, Pallas kernels for 0%

commit v1 on v0

v1 whole, which is shorter than its diff:
```python
import functools

import jax
import jax.numpy as jnp
from jax import lax
from jax.experimental import pallas as pl
from jax.experimental.pallas import tpu as pltpu
from jax.sharding import PartitionSpec as P

MESH = pl.DeviceIdType.MESH
GROUP = 4


def split(value):
    high = value.astype(jnp.bfloat16)
    low = (value - high.astype(jnp.float32)).astype(jnp.bfloat16)
    return high, low


def product(a_high, a_low, b_high, b_low):
    dims = (((1,), (1,)), ((), ()))
    dot = functools.partial(lax.dot_general, dimension_numbers=dims, preferred_element_type=jnp.float32)
    return dot(a_high, b_high) + (dot(a_high, b_low) + dot(a_low, b_high))


def kernel(
    planes, rows, width, samples,
    jac, out,
    own, high, low, other, sums, mean, part, core_in, y_in, x_in, near_in, far_in,
    copy_sem, swap_send, swap_recv, sum_send, sum_recv, line_send, line_recv,
    core_send, core_recv, y_send, y_recv, x_send, x_recv,
    near_send, near_recv, far_send, far_recv,
):
    half = width // 2
    per = planes // 2
    samp = lax.axis_index("samp")
    x = lax.axis_index("par")
    z = samp // GROUP
    q = samp % GROUP
    devices = planes * GROUP * 2
    me = samp * 2 + x

    def flip(a, k):
        low_a, high_a = a % 2, a // 2
        low_k, high_k = k % 2, k // 2
        return (low_a + low_k) % 2 + 2 * ((high_a + high_k) % 2)

    def remote(src, dst, send, recv, to_samp, to_par):
        return pltpu.make_async_remote_copy(
            src_ref=src, dst_ref=dst, send_sem=send, recv_sem=recv,
            device_id=(to_samp, to_par), device_id_type=MESH,
        )

    barrier = pltpu.get_barrier_semaphore()

    def greet(i, carry):
        @pl.when(i != me)
        def _():
            pl.semaphore_signal(barrier, inc=1, device_id=(i // 2, i % 2), device_id_type=MESH)
        return carry

    lax.fori_loop(0, devices, greet, 0)
    pl.semaphore_wait(barrier, devices - 1)

    def columns(i):
        return pl.ds(pl.multiple_of(i * width, width), width)

    def swap(k):
        to = flip(q, k)
        return remote(
            jac.at[:, columns(to)], own.at[q], swap_send.at[k], swap_recv.at[q], z * GROUP + to, x
        )

    def swap_in(k):
        return remote(
            jac.at[:, columns(q)], own.at[flip(q, k)], swap_send.at[k], swap_recv.at[flip(q, k)],
            z * GROUP + flip(q, k), x,
        )

    for k in (1, 2, 3):
        swap(k).start()
    mine = pltpu.make_async_copy(jac.at[:, columns(q)], own.at[q], copy_sem)
    mine.start()

    def left(plane, r, src):
        return remote(
            src, other.at[plane, r], line_send.at[0, plane, r], line_recv.at[plane, r],
            (z - 1) * GROUP + q, x,
        )

    def right(plane, r, src):
        return remote(
            src, other.at[plane, r], line_send.at[1, plane, r], line_recv.at[plane, r],
            (z + 1) * GROUP + q, x,
        )

    total = jnp.zeros((8, width), jnp.float32)
    for k in range(GROUP):
        r = flip(q, k)
        if k == 0:
            mine.wait()
        else:
            swap_in(k).wait_recv()

        @pl.when(z > 0)
        def _():
            left(z, r, own.at[r, :, pl.ds(0, half)]).start()

        @pl.when(z < planes - 1)
        def _():
            right(z, r, own.at[r, :, pl.ds(half, half)]).start()

        def add(i, acc):
            return acc + own[r, pl.ds(pl.multiple_of(i * 8, 8), 8), :]

        total = lax.fori_loop(0, rows // 8, add, total)
    sums[z] = total

    def sum_copy(plane, d):
        to = lax.rem(z + d, planes)
        return remote(
            sums.at[plane], sums.at[plane], sum_send.at[d], sum_recv.at[plane], to * GROUP + q, x
        )

    for d in range(1, planes):
        sum_copy(z, d).start()
    for d in range(1, planes):
        sum_copy(lax.rem(z + d, planes), d).wait_recv()
    whole = sums[0]
    for d in range(1, planes):
        whole = whole + sums[d]
    mean[...] = jnp.sum(whole, axis=0, keepdims=True) / samples

    @pl.loop(0, GROUP)
    def _(i):
        a, b = split(own[i] - mean[...])
        high[i] = a
        low[i] = b

    @pl.loop(0, GROUP * GROUP)
    def _(t):
        i, r = t // GROUP, t % GROUP
        part[z, i, r] = product(high[i], low[i], high[r], low[r])

    def multiply(plane, r, first):
        b_high, b_low = split(other[plane, r] - mean[:, pl.ds(first, half)])

        @pl.loop(0, GROUP)
        def _(i):
            part[plane, i, r] = product(
                high[i, :, pl.ds(first, half)], low[i, :, pl.ds(first, half)], b_high, b_low
            )

    def core_copy(plane, j):
        block = flip(q, 1 + 2 * j)
        return remote(
            part.at[plane, block], core_in.at[plane, j], core_send.at[plane, j],
            core_recv.at[plane, j], z * GROUP + flip(q, 1), x,
        )

    def y_copy(plane):
        return remote(
            part.at[plane, flip(q, 2)], y_in.at[plane], y_send.at[plane], y_recv.at[plane],
            z * GROUP + flip(q, 2), x,
        )

    def x_copy(plane):
        return remote(
            part.at[plane, q, pl.ds(2 * (1 - x), 2)], x_in.at[plane], x_send.at[plane],
            x_recv.at[plane], samp, 1 - x,
        )

    def near_copy(plane):
        return remote(
            part.at[plane, q, pl.ds(2 * x, 2)], near_in.at[plane % per], near_send.at[plane],
            near_recv.at[plane % per], samp, 1 - x,
        )

    def far_copy(plane, j):
        return remote(
            part.at[plane, q, 2 * x + j], far_in.at[z % per, q], far_send.at[plane, j],
            far_recv.at[z % per, q], plane * GROUP + 2 * x + j, z // per,
        )

    def stage0(plane):
        for j in (1, 0):
            core_copy(plane, j).start()

    def stage1(plane):
        core_copy(plane, 1).wait_recv()
        block = flip(q, 2)

        @pl.loop(0, GROUP)
        def _(r):
            part[plane, block, r] = part[plane, block, r] + core_in[plane, 1, r]

        y_copy(plane).start()
        core_copy(plane, 0).wait_recv()

        @pl.loop(0, GROUP)
        def _(r):
            part[plane, q, r] = part[plane, q, r] + core_in[plane, 0, r]

    def stage2(plane):
        y_copy(plane).wait_recv()

        @pl.loop(0, GROUP)
        def _(r):
            part[plane, q, r] = part[plane, q, r] + y_in[plane, r]

        x_copy(plane).start()

    def stage3(plane):
        x_copy(plane).wait_recv()
        for j in range(2):
            part[plane, q, 2 * x + j] = part[plane, q, 2 * x + j] + x_in[plane, j]

        @pl.when(plane // per != x)
        def _():
            near_copy(plane).start()

        @pl.when(plane != z)
        def _():
            for j in range(2):
                far_copy(plane, j).start()

    stages = (stage1, stage2, stage3)
    stage0(z)

    def step(t, carry):
        d, k = t // GROUP + 1, t % GROUP
        r = flip(q, k)
        before, after = z - d, z + d

        @pl.when(after < planes)
        def _():
            left(after, r, other.at[after, r]).wait_recv()

            @pl.when(z > 0)
            def _():
                left(after, r, other.at[after, r]).start()

        @pl.when(before >= 0)
        def _():
            right(before, r, other.at[before, r]).wait_recv()

            @pl.when(z < planes - 1)
            def _():
                right(before, r, other.at[before, r]).start()

        @pl.when(after < planes)
        def _():
            multiply(after, r, 0)

        @pl.when(before >= 0)
        def _():
            multiply(before, r, half)

        for i in range(3):
            @pl.when((k == i) & (d == 1))
            def _():
                stages[i](z)

            @pl.when((k == i) & (d > 1) & (after - 1 < planes))
            def _():
                stages[i](after - 1)

            @pl.when((k == i) & (d > 1) & (before + 1 >= 0))
            def _():
                stages[i](before + 1)

        @pl.when((k == GROUP - 1) & (after < planes))
        def _():
            stage0(after)

        @pl.when((k == GROUP - 1) & (before >= 0))
        def _():
            stage0(before)

        return carry

    lax.fori_loop(0, (planes - 1) * GROUP, step, 0)

    for last, exists in ((planes - 1, z == 0), (0, z == planes - 1)):
        @pl.when(exists)
        def _():
            for stage in stages:
                stage(last)

    for s in range(per):
        plane = x * per + s
        near_copy(plane).wait_recv()
        for r in range(GROUP):
            kept = part[plane, q, r]
            sent = near_in[s, r % 2]
            where = pl.ds((s * GROUP + r) * rows, rows)
            out[:, where] = jnp.where(x == r // 2, kept, sent) / samples

        @pl.when(plane != z)
        def _():
            for r in range(GROUP):
                remote(
                    part.at[plane, q, r], far_in.at[s, r], far_send.at[plane, 0], far_recv.at[s, r],
                    samp, 1 - x,
                ).wait_recv()
                where = pl.ds((s * GROUP + r) * rows, rows)
                out[:, where] = out[:, where] + far_in[s, r].T / samples

    for k in (1, 2, 3):
        swap(k).wait_send()
    for d in range(1, planes):
        sum_copy(z, d).wait_send()

    def drain(plane, carry):
        for r in range(GROUP):
            @pl.when((z > 0) & (plane >= z))
            def _():
                left(plane, r, other.at[plane, r]).wait_send()

            @pl.when((z < planes - 1) & (plane <= z))
            def _():
                right(plane, r, other.at[plane, r]).wait_send()

        for j in range(2):
            core_copy(plane, j).wait_send()
        y_copy(plane).wait_send()
        x_copy(plane).wait_send()

        @pl.when(plane // per != x)
        def _():
            near_copy(plane).wait_send()

        @pl.when(plane != z)
        def _():
            for j in range(2):
                far_copy(plane, j).wait_send()

        return carry

    lax.fori_loop(0, planes, drain, 0)


def lines(jacobian):
    rows, total = jacobian.shape
    count = lax.axis_size("samp")
    planes = count // GROUP
    per = planes // 2
    width = total // GROUP
    half = width // 2
    f32 = jnp.float32
    dma = pltpu.SemaphoreType.DMA
    body = functools.partial(kernel, planes, rows, width, float(rows * count))
    return pl.pallas_call(
        body,
        out_shape=jax.ShapeDtypeStruct((rows, per * GROUP * rows), f32),
        in_specs=[pl.BlockSpec(memory_space=pl.ANY)],
        out_specs=pl.BlockSpec(memory_space=pltpu.VMEM),
        scratch_shapes=[
            pltpu.VMEM((GROUP, rows, width), f32),
            pltpu.VMEM((GROUP, rows, width), jnp.bfloat16),
            pltpu.VMEM((GROUP, rows, width), jnp.bfloat16),
            pltpu.VMEM((planes, GROUP, rows, half), f32),
            pltpu.VMEM((planes, 8, width), f32),
            pltpu.VMEM((1, width), f32),
            pltpu.VMEM((planes, GROUP, GROUP, rows, rows), f32),
            pltpu.VMEM((planes, 2, GROUP, rows, rows), f32),
            pltpu.VMEM((planes, GROUP, rows, rows), f32),
            pltpu.VMEM((planes, 2, rows, rows), f32),
            pltpu.VMEM((per, 2, rows, rows), f32),
            pltpu.VMEM((per, GROUP, rows, rows), f32),
            dma,
            dma((GROUP,)), dma((GROUP,)),
            dma((planes,)), dma((planes,)),
            dma((2, planes, GROUP)), dma((planes, GROUP)),
            dma((planes, 2)), dma((planes, 2)),
            dma((planes,)), dma((planes,)),
            dma((planes,)), dma((planes,)),
            dma((planes,)), dma((per,)),
            dma((planes, 2)), dma((per, GROUP)),
        ],
        compiler_params=pltpu.CompilerParams(
            collective_id=0, has_side_effects=True, vmem_limit_bytes=60 * 2**20
        ),
    )(jacobian)


def tile_product(a, b):
    return jnp.dot(a, b.T, preferred_element_type=jnp.float32, precision=lax.Precision.HIGHEST)


def gathered(jacobian):
    rows = jacobian.shape[0]
    samples = rows * lax.axis_size("samp")
    totals = lax.psum(jnp.sum(jacobian, axis=0), "samp")
    centred = jacobian - (totals / samples)[None, :]
    partial_rows = tile_product(centred, lax.all_gather(centred, "samp", axis=0, tiled=True))
    return lax.psum_scatter(partial_rows, "par", scatter_dimension=1, tiled=True) / samples


def scratch_bytes(rows, total, planes):
    square = rows * rows * 4
    return rows * total * 4 * 2 + planes * rows * total * 2 + planes * square * 30 + planes * square * 5


def solution(mesh):
    planes, rest = divmod(mesh.shape["samp"], GROUP)

    def per_device(jacobian):
        rows, total = jacobian.shape
        fits = scratch_bytes(rows, total, planes) <= 56 * 2**20
        if mesh.shape["par"] == 2 and rest == 0 and planes % 2 == 0 and fits and total % 1024 == 0:
            return lines(jacobian)
        return gathered(jacobian)

    return jax.shard_map(
        per_device, mesh=mesh, in_specs=(P("samp", "par"),), out_specs=P("samp", "par"), check_vma=False
    )
```

time: 529 us -> 303 us (0.57)
  the two profiles are of different devices: /device:TPU:29 before, /device:TPU:3 now
where the time goes in v1:
time: 303 us
  Pallas kernels  300 us (99%)
  local copies, waits for them, and re-layouts  3.14 us (1%)
    pallas_call x1, Pallas kernels, lines(): pl.pallas_call(body, out_shape=jax.ShapeDtypeStruct((rows, per * GROUP *...  300 us

profile of v1, /device:TPU:3, one launch (start us, length us, event | category | flops | bytes accessed | tf_op | source)
XLA Modules:
  0.0 303.3 jit_solution(2125160232021660416)
XLA Ops:
  0.0 300.1 %shard_map.17 = f32[256,2048]{1,0:T(8,128)} custom-call(f32[256,4096]{1,0:T(8,128)} %jac.1), custom_call_target="tpu_custom_call" | custom-call | tf_op jit(solution)/shard_map/pallas_call | solution.py:353
  300.1 3.1 %copy.3 = f32[256,2048]{1,0:T(8,128)} copy(f32[256,2048]{1,0:T(8,128)} %shard_map.17) | data formatting | bytes 4194304

commit v2 on v1

v2 whole, which is shorter than its diff:
```python
import functools

import jax
import jax.numpy as jnp
from jax import lax
from jax.experimental import pallas as pl
from jax.experimental.pallas import tpu as pltpu
from jax.sharding import PartitionSpec as P

MESH = pl.DeviceIdType.MESH
GROUP = 4


def split(value):
    high = value.astype(jnp.bfloat16)
    low = (value - high.astype(jnp.float32)).astype(jnp.bfloat16)
    return high, low


def product(a_high, a_low, b_high, b_low):
    dims = (((1,), (1,)), ((), ()))
    dot = functools.partial(lax.dot_general, dimension_numbers=dims, preferred_element_type=jnp.float32)
    return dot(a_high, b_high) + (dot(a_high, b_low) + dot(a_low, b_high))


def kernel(
    planes, rows, width, samples,
    jac, out,
    own, high, low, other, sums, mean, part, core_in, y_in, x_in, near_in, far_in,
    copy_sem, swap_send, swap_recv, sum_send, sum_recv, line_send, line_recv,
    core_send, core_recv, y_send, y_recv, x_send, x_recv,
    near_send, near_recv, far_send, far_recv,
):
    half = width // 2
    per = planes // 2
    samp = lax.axis_index("samp")
    x = lax.axis_index("par")
    z = samp // GROUP
    q = samp % GROUP
    devices = planes * GROUP * 2
    me = samp * 2 + x

    def flip(a, k):
        low_a, high_a = a % 2, a // 2
        low_k, high_k = k % 2, k // 2
        return (low_a + low_k) % 2 + 2 * ((high_a + high_k) % 2)

    def remote(src, dst, send, recv, to_samp, to_par):
        return pltpu.make_async_remote_copy(
            src_ref=src, dst_ref=dst, send_sem=send, recv_sem=recv,
            device_id=(to_samp, to_par), device_id_type=MESH,
        )

    barrier = pltpu.get_barrier_semaphore()

    def greet(i, carry):
        @pl.when(i != me)
        def _():
            pl.semaphore_signal(barrier, inc=1, device_id=(i // 2, i % 2), device_id_type=MESH)
        return carry

    lax.fori_loop(0, devices, greet, 0)
    pl.semaphore_wait(barrier, devices - 1)

    def columns(i, h):
        return pl.ds(pl.multiple_of(i * width + h * half, half), half)

    def swap(k, h):
        to = flip(q, k)
        return remote(
            jac.at[:, columns(to, h)], own.at[h, q], swap_send.at[k, h], swap_recv.at[q, h],
            z * GROUP + to, x,
        )

    def swap_in(k, h):
        source = flip(q, k)
        return remote(
            jac.at[:, columns(q, h)], own.at[h, source], swap_send.at[k, h],
            swap_recv.at[source, h], z * GROUP + source, x,
        )

    mine = [
        pltpu.make_async_copy(jac.at[:, columns(q, h)], own.at[h, q], copy_sem.at[h]) for h in (0, 1)
    ]
    for k in range(GROUP):
        for h in (0, 1):
            if k == 0:
                mine[h].start()
            else:
                swap(k, h).start()

    def left(plane, r, src):
        return remote(
            src, other.at[plane, r], line_send.at[0, plane, r], line_recv.at[plane, r],
            (z - 1) * GROUP + q, x,
        )

    def right(plane, r, src):
        return remote(
            src, other.at[plane, r], line_send.at[1, plane, r], line_recv.at[plane, r],
            (z + 1) * GROUP + q, x,
        )

    totals = [jnp.zeros((8, half), jnp.float32) for _ in range(2)]
    for k in range(GROUP):
        r = flip(q, k)
        for h in (0, 1):
            if k == 0:
                mine[h].wait()
            else:
                swap_in(k, h).wait_recv()

            @pl.when((z > 0) if h == 0 else (z < planes - 1))
            def _():
                (left if h == 0 else right)(z, r, own.at[h, r]).start()

            def add(i, acc):
                return acc + own[h, r, pl.ds(pl.multiple_of(i * 8, 8), 8), :]

            totals[h] = lax.fori_loop(0, rows // 8, add, totals[h])
    for h in (0, 1):
        sums[z, h] = totals[h]

    def sum_copy(plane, d):
        to = lax.rem(z + d, planes)
        return remote(
            sums.at[plane], sums.at[plane], sum_send.at[d], sum_recv.at[plane], to * GROUP + q, x
        )

    for d in range(1, planes):
        sum_copy(z, d).start()

    def relay(d, r):
        before, after = z - d, z + d

        @pl.when(after < planes)
        def _():
            left(after, r, other.at[after, r]).wait_recv()

            @pl.when(z > 0)
            def _():
                left(after, r, other.at[after, r]).start()

        @pl.when(before >= 0)
        def _():
            right(before, r, other.at[before, r]).wait_recv()

            @pl.when(z < planes - 1)
            def _():
                right(before, r, other.at[before, r]).start()

    for r in range(GROUP):
        relay(1, r)

    for d in range(1, planes):
        sum_copy(lax.rem(z + d, planes), d).wait_recv()
    for h in (0, 1):
        whole = sums[0, h]
        for d in range(1, planes):
            whole = whole + sums[d, h]
        mean[h] = jnp.sum(whole, axis=0, keepdims=True) / samples

    @pl.loop(0, GROUP)
    def _(i):
        for h in (0, 1):
            a, b = split(own[h, i] - mean[h])
            high[h, i] = a
            low[h, i] = b

    def square(r):
        @pl.loop(0, GROUP)
        def _(i):
            part[z, i, r] = product(high[0, i], low[0, i], high[0, r], low[0, r]) + product(
                high[1, i], low[1, i], high[1, r], low[1, r]
            )

    def multiply(plane, r, h):
        b_high, b_low = split(other[plane, r] - mean[h])

        @pl.loop(0, GROUP)
        def _(i):
            part[plane, i, r] = product(high[h, i], low[h, i], b_high, b_low)

    def core_copy(plane, r, j):
        block = flip(q, 1 + 2 * j)
        return remote(
            part.at[plane, block, r], core_in.at[plane, r, j], core_send.at[plane, r, j],
            core_recv.at[plane, r, j], z * GROUP + flip(q, 1), x,
        )

    def y_copy(plane, r):
        return remote(
            part.at[plane, flip(q, 2), r], y_in.at[plane, r], y_send.at[plane, r],
            y_recv.at[plane, r], z * GROUP + flip(q, 2), x,
        )

    def x_copy(plane, r):
        return remote(
            part.at[plane, q, r], x_in.at[plane, r % 2], x_send.at[plane, r],
            x_recv.at[plane, r], samp, 1 - x,
        )

    def near_copy(plane, r):
        return remote(
            part.at[plane, q, r], near_in.at[plane % per, r % 2], near_send.at[plane, r],
            near_recv.at[plane % per, r % 2], samp, 1 - x,
        )

    def far_copy(plane, r):
        return remote(
            part.at[plane, q, r], far_in.at[z % per, q], far_send.at[plane, r],
            far_recv.at[z % per, q], plane * GROUP + r, z // per,
        )

    def stage0(plane, r):
        for j in (1, 0):
            core_copy(plane, r, j).start()

    def stage1(plane, r):
        core_copy(plane, r, 1).wait_recv()
        block = flip(q, 2)
        part[plane, block, r] = part[plane, block, r] + core_in[plane, r, 1]
        y_copy(plane, r).start()
        core_copy(plane, r, 0).wait_recv()
        part[plane, q, r] = part[plane, q, r] + core_in[plane, r, 0]

    def stage2(plane, r):
        y_copy(plane, r).wait_recv()
        part[plane, q, r] = part[plane, q, r] + y_in[plane, r]

        @pl.when(r // 2 != x)
        def _():
            x_copy(plane, r).start()

    def stage3(plane, r):
        @pl.when(r // 2 == x)
        def _():
            x_copy(plane, r).wait_recv()
            part[plane, q, r] = part[plane, q, r] + x_in[plane, r % 2]

            @pl.when(plane // per != x)
            def _():
                near_copy(plane, r).start()

            @pl.when(plane != z)
            def _():
                far_copy(plane, r).start()

    steps = planes * GROUP

    def each(e, run):
        d, r = e // GROUP, e % GROUP

        @pl.when((e >= 0) & (e < steps) & (z + d < planes))
        def _():
            run(z + d, r)

        @pl.when((e >= GROUP) & (e < steps) & (z - d >= 0))
        def _():
            run(z - d, r)

    def step(e, carry):
        d, r = e // GROUP, e % GROUP
        each(e - 3, stage3)
        each(e - 2, stage2)
        each(e - 1, stage1)

        @pl.when((d > 1) & (d < planes))
        def _():
            relay(d, r)

        @pl.when(d == 0)
        def _():
            square(r)

        @pl.when((d > 0) & (z + d < planes))
        def _():
            multiply(z + d, r, 0)

        @pl.when((d > 0) & (z - d >= 0))
        def _():
            multiply(z - d, r, 1)

        each(e, stage0)
        return carry

    lax.fori_loop(0, steps + 3, step, 0)

    for s in range(per):
        plane = x * per + s
        for j in range(2):
            near_copy(plane, j).wait_recv()
        for r in range(GROUP):
            kept = part[plane, q, r]
            sent = near_in[s, r % 2]
            where = pl.ds((s * GROUP + r) * rows, rows)
            out[:, where] = jnp.where(x == r // 2, kept, sent) / samples

        @pl.when(plane != z)
        def _():
            for r in range(GROUP):
                remote(
                    part.at[plane, q, r], far_in.at[s, r], far_send.at[plane, r], far_recv.at[s, r],
                    samp, 1 - x,
                ).wait_recv()
                where = pl.ds((s * GROUP + r) * rows, rows)
                out[:, where] = out[:, where] + far_in[s, r].T / samples

    for k in (1, 2, 3):
        for h in (0, 1):
            swap(k, h).wait_send()
    for d in range(1, planes):
        sum_copy(z, d).wait_send()

    def drain(t, carry):
        plane, r = t // GROUP, t % GROUP

        @pl.when((z > 0) & (plane >= z))
        def _():
            left(plane, r, other.at[plane, r]).wait_send()

        @pl.when((z < planes - 1) & (plane <= z))
        def _():
            right(plane, r, other.at[plane, r]).wait_send()

        for j in range(2):
            core_copy(plane, r, j).wait_send()
        y_copy(plane, r).wait_send()

        @pl.when(r // 2 != x)
        def _():
            x_copy(plane, r).wait_send()

        @pl.when((r // 2 == x) & (plane // per != x))
        def _():
            near_copy(plane, r).wait_send()

        @pl.when((r // 2 == x) & (plane != z))
        def _():
            far_copy(plane, r).wait_send()

        return carry

    lax.fori_loop(0, steps, drain, 0)


def lines(jacobian):
    rows, total = jacobian.shape
    count = lax.axis_size("samp")
    planes = count // GROUP
    per = planes // 2
    width = total // GROUP
    half = width // 2
    f32 = jnp.float32
    dma = pltpu.SemaphoreType.DMA
    body = functools.partial(kernel, planes, rows, width, float(rows * count))
    return pl.pallas_call(
        body,
        out_shape=jax.ShapeDtypeStruct((rows, per * GROUP * rows), f32),
        in_specs=[pl.BlockSpec(memory_space=pl.ANY)],
        out_specs=pl.BlockSpec(memory_space=pltpu.VMEM),
        scratch_shapes=[
            pltpu.VMEM((2, GROUP, rows, half), f32),
            pltpu.VMEM((2, GROUP, rows, half), jnp.bfloat16),
            pltpu.VMEM((2, GROUP, rows, half), jnp.bfloat16),
            pltpu.VMEM((planes, GROUP, rows, half), f32),
            pltpu.VMEM((planes, 2, 8, half), f32),
            pltpu.VMEM((2, 1, half), f32),
            pltpu.VMEM((planes, GROUP, GROUP, rows, rows), f32),
            pltpu.VMEM((planes, GROUP, 2, rows, rows), f32),
            pltpu.VMEM((planes, GROUP, rows, rows), f32),
            pltpu.VMEM((planes, 2, rows, rows), f32),
            pltpu.VMEM((per, 2, rows, rows), f32),
            pltpu.VMEM((per, GROUP, rows, rows), f32),
            dma((2,)),
            dma((GROUP, 2)), dma((GROUP, 2)),
            dma((planes,)), dma((planes,)),
            dma((2, planes, GROUP)), dma((planes, GROUP)),
            dma((planes, GROUP, 2)), dma((planes, GROUP, 2)),
            dma((planes, GROUP)), dma((planes, GROUP)),
            dma((planes, GROUP)), dma((planes, GROUP)),
            dma((planes, GROUP)), dma((per, 2)),
            dma((planes, GROUP)), dma((per, GROUP)),
        ],
        compiler_params=pltpu.CompilerParams(
            collective_id=0, has_side_effects=True, vmem_limit_bytes=60 * 2**20
        ),
    )(jacobian)


def tile_product(a, b):
    return jnp.dot(a, b.T, preferred_element_type=jnp.float32, precision=lax.Precision.HIGHEST)


def gathered(jacobian):
    rows = jacobian.shape[0]
    samples = rows * lax.axis_size("samp")
    totals = lax.psum(jnp.sum(jacobian, axis=0), "samp")
    centred = jacobian - (totals / samples)[None, :]
    partial_rows = tile_product(centred, lax.all_gather(centred, "samp", axis=0, tiled=True))
    return lax.psum_scatter(partial_rows, "par", scatter_dimension=1, tiled=True) / samples


def scratch_bytes(rows, total, planes):
    square = rows * rows * 4
    return rows * total * 4 * 2 + planes * rows * total * 2 + planes * square * 30 + planes * square * 5


def solution(mesh):
    planes, rest = divmod(mesh.shape["samp"], GROUP)

    def per_device(jacobian):
        rows, total = jacobian.shape
        fits = scratch_bytes(rows, total, planes) <= 56 * 2**20
        if mesh.shape["par"] == 2 and rest == 0 and planes % 2 == 0 and fits and total % 1024 == 0:
            return lines(jacobian)
        return gathered(jacobian)

    return jax.shard_map(
        per_device, mesh=mesh, in_specs=(P("samp", "par"),), out_specs=P("samp", "par"), check_vma=False
    )
```

time: 303 us -> 274 us (0.904)
  the two profiles are of different devices: /device:TPU:3 before, /device:TPU:29 now
where the time goes in v2:
time: 274 us
  Pallas kernels  271 us (99%)
  local copies, waits for them, and re-layouts  3.14 us (1%)
    pallas_call x1, Pallas kernels, lines(): pl.pallas_call(body, out_shape=jax.ShapeDtypeStruct((rows, per * GROUP *...  271 us

profile of v2, /device:TPU:29, one launch (start us, length us, event | category | flops | bytes accessed | tf_op | source)
XLA Modules:
  0.0 274.1 jit_solution(362678628718694103)
XLA Ops:
  0.0 270.9 %shard_map.17 = f32[256,2048]{1,0:T(8,128)} custom-call(f32[256,4096]{1,0:T(8,128)} %jac.1), custom_call_target="tpu_custom_call" | custom-call | tf_op jit(solution)/shard_map/pallas_call | solution.py:357
  271.0 3.1 %copy.3 = f32[256,2048]{1,0:T(8,128)} copy(f32[256,2048]{1,0:T(8,128)} %shard_map.17) | data formatting | bytes 4194304

commit v3 on v2

--- a/solution.py
+++ b/solution.py
@@ -194,10 +194,10 @@
             y_recv.at[plane, r], z * GROUP + flip(q, 2), x,
         )
 
-    def x_copy(plane, r):
-        return remote(
-            part.at[plane, q, r], x_in.at[plane, r % 2], x_send.at[plane, r],
-            x_recv.at[plane, r], samp, 1 - x,
+    def x_copy(plane, r, j):
+        return remote(
+            part.at[plane, flip(q, 2 * j), r], x_in.at[plane, r % 2 + j], x_send.at[plane, r, j],
+            x_recv.at[plane, r, j], samp, 1 - x,
         )
 
     def near_copy(plane, r):
@@ -215,28 +215,61 @@
     def stage0(plane, r):
         for j in (1, 0):
             core_copy(plane, r, j).start()
+
+    def add_y(plane, r):
+        y_copy(plane, r).wait_recv()
+        part[plane, q, r] = part[plane, q, r] + y_in[plane, r]
+
+    def add_x(plane, r, j):
+        x_copy(plane, r, j).wait_recv()
+        block = flip(q, 2 * j)
+        part[plane, block, r] = part[plane, block, r] + x_in[plane, r % 2 + j]
 
     def stage1(plane, r):
         core_copy(plane, r, 1).wait_recv()
         block = flip(q, 2)
         part[plane, block, r] = part[plane, block, r] + core_in[plane, r, 1]
-        y_copy(plane, r).start()
+
+        @pl.when(r % 2 == 0)
+        def _():
+            y_copy(plane, r).start()
+
+        @pl.when((r % 2 == 1) & (r // 2 != x))
+        def _():
+            x_copy(plane, r, 1).start()
+
         core_copy(plane, r, 0).wait_recv()
         part[plane, q, r] = part[plane, q, r] + core_in[plane, r, 0]
 
+        @pl.when((r % 2 == 1) & (r // 2 != x))
+        def _():
+            x_copy(plane, r, 0).start()
+
     def stage2(plane, r):
-        y_copy(plane, r).wait_recv()
-        part[plane, q, r] = part[plane, q, r] + y_in[plane, r]
-
-        @pl.when(r // 2 != x)
-        def _():
-            x_copy(plane, r).start()
+        @pl.when(r % 2 == 0)
+        def _():
+            add_y(plane, r)
+
+            @pl.when(r // 2 != x)
+            def _():
+                x_copy(plane, r, 0).start()
+
+        @pl.when((r % 2 == 1) & (r // 2 == x))
+        def _():
+            add_x(plane, r, 1)
+            y_copy(plane, r).start()
+            add_x(plane, r, 0)
 
     def stage3(plane, r):
         @pl.when(r // 2 == x)
         def _():
-            x_copy(plane, r).wait_recv()
-            part[plane, q, r] = part[plane, q, r] + x_in[plane, r % 2]
+            @pl.when(r % 2 == 0)
+            def _():
+                add_x(plane, r, 0)
+
+            @pl.when(r % 2 == 1)
+            def _():
+                add_y(plane, r)
 
             @pl.when(plane // per != x)
             def _():
@@ -261,13 +294,17 @@
 
     def step(e, carry):
         d, r = e // GROUP, e % GROUP
+        for block in range(GROUP):
+            early = 2 * GROUP - 1 - block // 2
+            ahead = (e + early) // GROUP
+
+            @pl.when(((e + early) % GROUP == block) & (ahead > 1) & (ahead < planes))
+            def _():
+                relay(ahead, block)
+
         each(e - 3, stage3)
         each(e - 2, stage2)
         each(e - 1, stage1)
-
-        @pl.when((d > 1) & (d < planes))
-        def _():
-            relay(d, r)
 
         @pl.when(d == 0)
         def _():
@@ -325,11 +362,18 @@
 
         for j in range(2):
             core_copy(plane, r, j).wait_send()
-        y_copy(plane, r).wait_send()
+
+        @pl.when((r % 2 == 0) | (r // 2 == x))
+        def _():
+            y_copy(plane, r).wait_send()
 
         @pl.when(r // 2 != x)
         def _():
-            x_copy(plane, r).wait_send()
+            x_copy(plane, r, 0).wait_send()
+
+            @pl.when(r % 2 == 1)
+            def _():
+                x_copy(plane, r, 1).wait_send()
 
         @pl.when((r // 2 == x) & (plane // per != x))
         def _():
@@ -369,7 +413,7 @@
             pltpu.VMEM((planes, GROUP, GROUP, rows, rows), f32),
             pltpu.VMEM((planes, GROUP, 2, rows, rows), f32),
             pltpu.VMEM((planes, GROUP, rows, rows), f32),
-            pltpu.VMEM((planes, 2, rows, rows), f32),
+            pltpu.VMEM((planes, 3, rows, rows), f32),
             pltpu.VMEM((per, 2, rows, rows), f32),
             pltpu.VMEM((per, GROUP, rows, rows), f32),
             dma((2,)),
@@ -378,7 +422,7 @@
             dma((2, planes, GROUP)), dma((planes, GROUP)),
             dma((planes, GROUP, 2)), dma((planes, GROUP, 2)),
             dma((planes, GROUP)), dma((planes, GROUP)),
-            dma((planes, GROUP)), dma((planes, GROUP)),
+            dma((planes, GROUP, 2)), dma((planes, GROUP, 2)),
             dma((planes, GROUP)), dma((per, 2)),
             dma((planes, GROUP)), dma((per, GROUP)),
         ],

time: 274 us -> 326 us (1.19)
  Pallas kernels: 271 us -> 323 us
    pallas_call x1, Pallas kernels: 271 us -> 323 us  [lines(): pl.pallas_call(body, out_shape=jax.ShapeDtypeStruct((rows, per * GROUP *...]
where the time goes in v3:
time: 326 us
  Pallas kernels  323 us (99%)
    pallas_call x1, Pallas kernels, lines(): pl.pallas_call(body, out_shape=jax.ShapeDtypeStruct((rows, per * GROUP *...  323 us

profile of v3, /device:TPU:29, one launch (start us, length us, event | category | flops | bytes accessed | tf_op | source)
XLA Modules:
  0.0 326.0 jit_solution(17154841188049400625)
XLA Ops:
  0.0 322.9 %shard_map.17 = f32[256,2048]{1,0:T(8,128)} custom-call(f32[256,4096]{1,0:T(8,128)} %jac.1), custom_call_target="tpu_custom_call" | custom-call | tf_op jit(solution)/shard_map/pallas_call | solution.py:401
  322.9 3.1 copy.3

commit v4 on v3

--- a/solution.py
+++ b/solution.py
@@ -130,27 +130,23 @@
     for d in range(1, planes):
         sum_copy(z, d).start()
 
-    def relay(d, r):
+    def relay(d, r, passes):
         before, after = z - d, z + d
 
-        @pl.when(after < planes)
+        @pl.when((after < planes) & ((z > 0) == passes))
         def _():
             left(after, r, other.at[after, r]).wait_recv()
-
-            @pl.when(z > 0)
-            def _():
+            if passes:
                 left(after, r, other.at[after, r]).start()
 
-        @pl.when(before >= 0)
+        @pl.when((before >= 0) & ((z < planes - 1) == passes))
         def _():
             right(before, r, other.at[before, r]).wait_recv()
-
-            @pl.when(z < planes - 1)
-            def _():
+            if passes:
                 right(before, r, other.at[before, r]).start()
 
     for r in range(GROUP):
-        relay(1, r)
+        relay(1, r, True)
 
     for d in range(1, planes):
         sum_copy(lax.rem(z + d, planes), d).wait_recv()
@@ -300,11 +296,15 @@
 
             @pl.when(((e + early) % GROUP == block) & (ahead > 1) & (ahead < planes))
             def _():
-                relay(ahead, block)
+                relay(ahead, block, True)
 
         each(e - 3, stage3)
         each(e - 2, stage2)
         each(e - 1, stage1)
+
+        @pl.when((d > 0) & (d < planes))
+        def _():
+            relay(d, r, False)
 
         @pl.when(d == 0)
         def _():

time: 326 us -> 318 us (0.975)
  Pallas kernels: 323 us -> 315 us
    pallas_call x1, Pallas kernels: 323 us -> 315 us  [lines(): pl.pallas_call(body, out_shape=jax.ShapeDtypeStruct((rows, per * GROUP *...]
where the time goes in v4:
time: 318 us
  Pallas kernels  315 us (99%)
    pallas_call x1, Pallas kernels, lines(): pl.pallas_call(body, out_shape=jax.ShapeDtypeStruct((rows, per * GROUP *...  315 us

profile of v4, /device:TPU:29, one launch (start us, length us, event | category | flops | bytes accessed | tf_op | source)
XLA Modules:
  0.0 318.2 jit_solution(17336736154158761640)
XLA Ops:
  0.0 315.1 %shard_map.17 = f32[256,2048]{1,0:T(8,128)} custom-call(f32[256,4096]{1,0:T(8,128)} %jac.1), custom_call_target="tpu_custom_call" | custom-call | tf_op jit(solution)/shard_map/pallas_call | solution.py:401
  315.1 3.1 copy.3

commit v5 on v2

--- a/solution.py
+++ b/solution.py
@@ -130,27 +130,23 @@
     for d in range(1, planes):
         sum_copy(z, d).start()
 
-    def relay(d, r):
+    def relay(d, r, passes):
         before, after = z - d, z + d
 
-        @pl.when(after < planes)
+        @pl.when((after < planes) & ((z > 0) == passes))
         def _():
             left(after, r, other.at[after, r]).wait_recv()
-
-            @pl.when(z > 0)
-            def _():
+            if passes:
                 left(after, r, other.at[after, r]).start()
 
-        @pl.when(before >= 0)
+        @pl.when((before >= 0) & ((z < planes - 1) == passes))
         def _():
             right(before, r, other.at[before, r]).wait_recv()
-
-            @pl.when(z < planes - 1)
-            def _():
+            if passes:
                 right(before, r, other.at[before, r]).start()
 
     for r in range(GROUP):
-        relay(1, r)
+        relay(1, r, True)
 
     for d in range(1, planes):
         sum_copy(lax.rem(z + d, planes), d).wait_recv()
@@ -261,13 +257,17 @@
 
     def step(e, carry):
         d, r = e // GROUP, e % GROUP
+        @pl.when((d > 0) & (d + 1 < planes))
+        def _():
+            relay(d + 1, r, True)
+
         each(e - 3, stage3)
         each(e - 2, stage2)
         each(e - 1, stage1)
 
-        @pl.when((d > 1) & (d < planes))
-        def _():
-            relay(d, r)
+        @pl.when((d > 0) & (d < planes))
+        def _():
+            relay(d, r, False)
 
         @pl.when(d == 0)
         def _():

time: 274 us -> 254 us (0.927); the launches traced: 274 us -> 250 us
  Pallas kernels: 271 us -> 247 us
    pallas_call x1, Pallas kernels: 271 us -> 247 us  [lines(): pl.pallas_call(body, out_shape=jax.ShapeDtypeStruct((rows, per * GROUP *...]
where the time goes in v5:
time: 254 us; the launch traced here: 250 us
  Pallas kernels  247 us (97%)
  local copies, waits for them, and re-layouts  3.14 us (1%)
    pallas_call x1, Pallas kernels, lines(): pl.pallas_call(body, out_shape=jax.ShapeDtypeStruct((rows, per * GROUP *...  247 us

profile of v5, /device:TPU:29, one launch (start us, length us, event | category | flops | bytes accessed | tf_op | source)
XLA Modules:
  0.0 250.2 jit_solution(17611914852882464880)
XLA Ops:
  0.0 247.1 %shard_map.17 = f32[256,2048]{1,0:T(8,128)} custom-call(f32[256,4096]{1,0:T(8,128)} %jac.1), custom_call_target="tpu_custom_call" | custom-call | tf_op jit(solution)/shard_map/pallas_call | solution.py:357
  247.1 3.1 %copy.3 = f32[256,2048]{1,0:T(8,128)} copy(f32[256,2048]{1,0:T(8,128)} %shard_map.17) | data formatting | bytes 4194304

commit v6 on v5

--- a/solution.py
+++ b/solution.py
@@ -82,13 +82,6 @@
     mine = [
         pltpu.make_async_copy(jac.at[:, columns(q, h)], own.at[h, q], copy_sem.at[h]) for h in (0, 1)
     ]
-    for k in range(GROUP):
-        for h in (0, 1):
-            if k == 0:
-                mine[h].start()
-            else:
-                swap(k, h).start()
-
     def left(plane, r, src):
         return remote(
             src, other.at[plane, r], line_send.at[0, plane, r], line_recv.at[plane, r],
@@ -100,6 +93,25 @@
             src, other.at[plane, r], line_send.at[1, plane, r], line_recv.at[plane, r],
             (z + 1) * GROUP + q, x,
         )
+
+    def send_own(r, sources):
+        @pl.when(z > 0)
+        def _():
+            left(z, r, sources[0]).start()
+
+        @pl.when(z < planes - 1)
+        def _():
+            right(z, r, sources[1]).start()
+
+    def send_swap(k):
+        for h in (0, 1):
+            swap(k, h).start()
+
+    for h in (0, 1):
+        mine[h].start()
+    send_swap(1)
+    send_own(q, [jac.at[:, columns(q, h)] for h in (0, 1)])
+    send_swap(2)
 
     totals = [jnp.zeros((8, half), jnp.float32) for _ in range(2)]
     for k in range(GROUP):
@@ -110,10 +122,14 @@
             else:
                 swap_in(k, h).wait_recv()
 
-            @pl.when((z > 0) if h == 0 else (z < planes - 1))
-            def _():
-                (left if h == 0 else right)(z, r, own.at[h, r]).start()
-
+            if k > 0:
+                @pl.when((z > 0) if h == 0 else (z < planes - 1))
+                def _():
+                    (left if h == 0 else right)(z, r, own.at[h, r]).start()
+
+        if k == 1:
+            send_swap(3)
+        for h in (0, 1):
             def add(i, acc):
                 return acc + own[h, r, pl.ds(pl.multiple_of(i * 8, 8), 8), :]
 
@@ -261,9 +277,12 @@
         def _():
             relay(d + 1, r, True)
 
-        each(e - 3, stage3)
-        each(e - 2, stage2)
-        each(e - 1, stage1)
+        each(e - 5, stage3)
+        each(e - 3, stage2)
+
+        @pl.when(e > 2 * GROUP)
+        def _():
+            each(e - 1, stage1)
 
         @pl.when((d > 0) & (d < planes))
         def _():
@@ -282,9 +301,14 @@
             multiply(z - d, r, 1)
 
         each(e, stage0)
+
+        @pl.when(e <= 2 * GROUP)
+        def _():
+            each(e - 1, stage1)
+
         return carry
 
-    lax.fori_loop(0, steps + 3, step, 0)
+    lax.fori_loop(0, steps + 5, step, 0)
 
     for s in range(per):
         plane = x * per + s

time: 254 us -> 222 us (0.87); the launches traced: 250 us -> 222 us
  Pallas kernels: 247 us -> 219 us
    pallas_call x1, Pallas kernels: 247 us -> 219 us  [lines(): pl.pallas_call(body, out_shape=jax.ShapeDtypeStruct((rows, per * GROUP *...]
where the time goes in v6:
time: 222 us
  Pallas kernels  219 us (99%)
  local copies, waits for them, and re-layouts  3.14 us (1%)
    pallas_call x1, Pallas kernels, lines(): pl.pallas_call(body, out_shape=jax.ShapeDtypeStruct((rows, per * GROUP *...  219 us

profile of v6, /device:TPU:29, one launch (start us, length us, event | category | flops | bytes accessed | tf_op | source)
XLA Modules:
  0.0 221.9 jit_solution(11972171282515127397)
XLA Ops:
  0.0 218.7 %shard_map.17 = f32[256,2048]{1,0:T(8,128)} custom-call(f32[256,4096]{1,0:T(8,128)} %jac.1), custom_call_target="tpu_custom_call" | custom-call | tf_op jit(solution)/shard_map/pallas_call | solution.py:381
  218.7 3.1 %copy.3 = f32[256,2048]{1,0:T(8,128)} copy(f32[256,2048]{1,0:T(8,128)} %shard_map.17) | data formatting | bytes 4194304

commit v7 on v4

--- a/solution.py
+++ b/solution.py
@@ -82,13 +82,6 @@
     mine = [
         pltpu.make_async_copy(jac.at[:, columns(q, h)], own.at[h, q], copy_sem.at[h]) for h in (0, 1)
     ]
-    for k in range(GROUP):
-        for h in (0, 1):
-            if k == 0:
-                mine[h].start()
-            else:
-                swap(k, h).start()
-
     def left(plane, r, src):
         return remote(
             src, other.at[plane, r], line_send.at[0, plane, r], line_recv.at[plane, r],
@@ -100,6 +93,25 @@
             src, other.at[plane, r], line_send.at[1, plane, r], line_recv.at[plane, r],
             (z + 1) * GROUP + q, x,
         )
+
+    def send_own(r, sources):
+        @pl.when(z > 0)
+        def _():
+            left(z, r, sources[0]).start()
+
+        @pl.when(z < planes - 1)
+        def _():
+            right(z, r, sources[1]).start()
+
+    def send_swap(k):
+        for h in (0, 1):
+            swap(k, h).start()
+
+    for h in (0, 1):
+        mine[h].start()
+    send_swap(1)
+    send_own(q, [jac.at[:, columns(q, h)] for h in (0, 1)])
+    send_swap(2)
 
     totals = [jnp.zeros((8, half), jnp.float32) for _ in range(2)]
     for k in range(GROUP):
@@ -110,10 +122,14 @@
             else:
                 swap_in(k, h).wait_recv()
 
-            @pl.when((z > 0) if h == 0 else (z < planes - 1))
-            def _():
-                (left if h == 0 else right)(z, r, own.at[h, r]).start()
-
+            if k > 0:
+                @pl.when((z > 0) if h == 0 else (z < planes - 1))
+                def _():
+                    (left if h == 0 else right)(z, r, own.at[h, r]).start()
+
+        if k == 1:
+            send_swap(3)
+        for h in (0, 1):
             def add(i, acc):
                 return acc + own[h, r, pl.ds(pl.multiple_of(i * 8, 8), 8), :]
 
@@ -290,17 +306,16 @@
 
     def step(e, carry):
         d, r = e // GROUP, e % GROUP
-        for block in range(GROUP):
-            early = 2 * GROUP - 1 - block // 2
-            ahead = (e + early) // GROUP
-
-            @pl.when(((e + early) % GROUP == block) & (ahead > 1) & (ahead < planes))
-            def _():
-                relay(ahead, block, True)
-
-        each(e - 3, stage3)
-        each(e - 2, stage2)
-        each(e - 1, stage1)
+        @pl.when((d > 0) & (d + 1 < planes))
+        def _():
+            relay(d + 1, r, True)
+
+        each(e - 5, stage3)
+        each(e - 3, stage2)
+
+        @pl.when(e > 2 * GROUP)
+        def _():
+            each(e - 1, stage1)
 
         @pl.when((d > 0) & (d < planes))
         def _():
@@ -319,9 +334,14 @@
             multiply(z - d, r, 1)
 
         each(e, stage0)
+
+        @pl.when(e <= 2 * GROUP)
+        def _():
+            each(e - 1, stage1)
+
         return carry
 
-    lax.fori_loop(0, steps + 3, step, 0)
+    lax.fori_loop(0, steps + 5, step, 0)
 
     for s in range(per):
         plane = x * per + s

time: 318 us -> 240 us (0.75)
  Pallas kernels: 315 us -> 236 us
    pallas_call x1, Pallas kernels: 315 us -> 236 us  [lines(): pl.pallas_call(body, out_shape=jax.ShapeDtypeStruct((rows, per * GROUP *...]
where the time goes in v7:
time: 240 us; the launch traced here: 239 us
  Pallas kernels  236 us (98%)
  local copies, waits for them, and re-layouts  3.14 us (1%)
    pallas_call x1, Pallas kernels, lines(): pl.pallas_call(body, out_shape=jax.ShapeDtypeStruct((rows, per * GROUP *...  236 us

profile of v7, /device:TPU:29, one launch (start us, length us, event | category | flops | bytes accessed | tf_op | source)
XLA Modules:
  0.0 239.4 jit_solution(16376136860189667059)
XLA Ops:
  0.0 236.2 %shard_map.17 = f32[256,2048]{1,0:T(8,128)} custom-call(f32[256,4096]{1,0:T(8,128)} %jac.1), custom_call_target="tpu_custom_call" | custom-call | tf_op jit(solution)/shard_map/pallas_call | solution.py:421
  236.2 3.1 %copy.3 = f32[256,2048]{1,0:T(8,128)} copy(f32[256,2048]{1,0:T(8,128)} %shard_map.17) | data formatting | bytes 4194304

commit v8 on v6

--- a/solution.py
+++ b/solution.py
@@ -273,10 +273,6 @@
 
     def step(e, carry):
         d, r = e // GROUP, e % GROUP
-        @pl.when((d > 0) & (d + 1 < planes))
-        def _():
-            relay(d + 1, r, True)
-
         each(e - 5, stage3)
         each(e - 3, stage2)
 
@@ -301,6 +297,10 @@
             multiply(z - d, r, 1)
 
         each(e, stage0)
+
+        @pl.when((d > 0) & (d + 1 < planes))
+        def _():
+            relay(d + 1, r, True)
 
         @pl.when(e <= 2 * GROUP)
         def _():

time: 222 us -> 222 us (level)
  no operation moved by 1% of the time
where the time goes in v8:
time: 222 us
  Pallas kernels  219 us (99%)
  local copies, waits for them, and re-layouts  3.14 us (1%)
    pallas_call x1, Pallas kernels, lines(): pl.pallas_call(body, out_shape=jax.ShapeDtypeStruct((rows, per * GROUP *...  219 us

profile of v8, /device:TPU:29, one launch (start us, length us, event | category | flops | bytes accessed | tf_op | source)
XLA Modules:
  0.0 221.9 jit_solution(13600133850150311455)
XLA Ops:
  0.0 218.7 %shard_map.17 = f32[256,2048]{1,0:T(8,128)} custom-call(f32[256,4096]{1,0:T(8,128)} %jac.1), custom_call_target="tpu_custom_call" | custom-call | tf_op jit(solution)/shard_map/pallas_call | solution.py:381
  218.7 3.1 %copy.3 = f32[256,2048]{1,0:T(8,128)} copy(f32[256,2048]{1,0:T(8,128)} %shard_map.17) | data formatting | bytes 4194304
